TPU v7x, 32 devices: a whole 2x2x4 slice. The times are simulated.
32 devices in a mesh: dp: 2 (over y), corpus: 4 (over x, core), tensor: 4 (over z).
Axes of the slice: x: 2, y: 2, z: 4, core: 2. Of those that a mesh axis runs over, the one named last changes fastest.
Arguments:
- hidden: bfloat16 [4096, 4096], P(('dp', 'corpus')), may hold values from -6 to 6
- norm_gain: bfloat16 [4096], replicated, may hold values from 0.099609375 to 1.8984375
- query_weight: bfloat16 [4096, 4096], P('corpus', 'tensor'), may hold values from -0.1875 to 0.1875
- output_weight: bfloat16 [4096, 4096], P('tensor'), may hold values from -0.375 to 0.375
- cache: bfloat16 [2, 8192, 1024], P(None, 'corpus', 'tensor'), may hold values from -240 to 240
- pattern: int32 [32, 16], P(('dp', 'corpus')), may hold values from 0 to 63, as said below
Outputs:
- scored: bfloat16 [4096, 4096], P(('dp', 'corpus', 'tensor'))
Inputs may be any that keep to these rules, and one draw needn't show every extreme that they name: Passage block j lies on index j // 16 of corpus. The 4 rows of pattern of one index of dp and corpus name blocks of exactly half of the indices of corpus, each of those exactly 32 times, repeats counted.
All inputs are finite; a program needn't handle non-finite values.
Results may differ from a plain program's by a relative error of at most 0.0075.
The roundings to bfloat16 on the way count: a program that leaves them out, or rounds other values in their place, can miss the bound.
Values may be sent and summed in bfloat16 or wider, within the bound.
A program may use at most 128 MiB of HBM per device.

v0:
```python
import math

import jax
import jax.numpy as jnp
from jax import lax
from jax.sharding import PartitionSpec as P

HD = 128
BLOCK = 128


def per_device(hidden, norm_gain, query_weight, output_weight, cache, pattern):
    widened = hidden.astype(jnp.float32)
    meansq = jnp.mean(widened * widened, axis=-1, keepdims=True)
    normed = (widened * lax.rsqrt(meansq + 1e-05) * norm_gain.astype(jnp.float32)).astype(
        jnp.bfloat16
    )
    projected = jnp.dot(
        normed,
        lax.all_gather(query_weight, "corpus", axis=0, tiled=True),
        preferred_element_type=jnp.float32,
    )
    queries = (projected * (1.0 / math.sqrt(HD))).astype(jnp.bfloat16)
    kv_width = cache.shape[2]
    kv_heads = kv_width // HD
    head_local = query_weight.shape[1] // HD
    group_size = head_local // kv_heads
    query_blocks = pattern.shape[0]
    slot_total = query_blocks * pattern.shape[1]
    whole = lax.all_gather(cache, "corpus", axis=1, tiled=True)
    tiles = whole.reshape(2, whole.shape[1] // BLOCK, BLOCK, kv_width)
    picked = jnp.take(tiles, pattern.reshape(slot_total), axis=1)
    key_span = pattern.shape[1] * BLOCK
    keys_here = picked[0].reshape(query_blocks, key_span, kv_heads, HD)
    values_here = picked[1].reshape(query_blocks, key_span, kv_heads, HD)
    query_tiles = queries.reshape(query_blocks, BLOCK, kv_heads, group_size, HD)
    scores = jnp.einsum(
        "qrkgd,qskd->qkgrs", query_tiles, keys_here, preferred_element_type=jnp.float32
    )
    highest = jnp.max(scores, axis=-1, keepdims=True)
    weights = jnp.exp(scores - highest)
    totals = jnp.sum(weights, axis=-1, keepdims=True)
    probs = weights.astype(jnp.bfloat16)
    mixed = (
        jnp.einsum("qkgrs,qskd->qkgrd", probs, values_here, preferred_element_type=jnp.float32)
        / totals
    )
    attended = (
        jnp.transpose(mixed, (0, 3, 1, 2, 4))
        .reshape(query_blocks * BLOCK, head_local * HD)
        .astype(jnp.bfloat16)
    )
    summed = lax.psum_scatter(
        jnp.dot(attended, output_weight, preferred_element_type=jnp.float32),
        "tensor",
        scatter_dimension=0,
        tiled=True,
    )
    return summed.astype(jnp.bfloat16)


def solution(mesh):
    in_specs = (
        P(("dp", "corpus"), None),
        P(),
        P("corpus", "tensor"),
        P("tensor", None),
        P(None, "corpus", "tensor"),
        P(("dp", "corpus"), None),
    )
    out_specs = P(("dp", "corpus", "tensor"), None)
    return jax.shard_map(
        per_device, mesh=mesh, in_specs=in_specs, out_specs=out_specs, check_vma=False
    )
```

profile of v0, /device:TPU:17, one launch (start us, length us, event | category | flops | bytes accessed | tf_op | source)
XLA Modules:
  0.0 355.2 jit_solution(3766558411114067843)
XLA Ops:
  6.5 0.0 all-gather.3.cloned.1.call-start
  6.5 0.7 all-gather.3.cloned.1.call-update
  7.3 0.0 all-gather.5.cloned.1.call-start
  7.3 0.7 all-gather.5.cloned.1.call-update
  8.0 0.0 reduce-scatter.2.cloned.1.call-start
  8.1 0.8 reshape.60
  8.8 0.8 reshape.58
  9.6 0.7 convert_element_type.25
  10.3 3.1 fusion.6
  13.4 55.3 %all-gather.3.cloned.1.call-done = bf16[2,8192,256]{2,1,0:T(8,128)(2,1)} async-done(((bf16[2,2048,256]{2,1,0:T(8,128)(2,1)}), bf16[2,8192,256]{2,1,0:T(8,128)(2,1)}) %all-gather.3.cloned.1.call-update) | async-done | bytes 8388624 | tf_op jit(solution)/shard_map/all_gather | solution.py:30
  68.7 9.1 %gather_fusion = bf16[64,2,128,256]{3,2,1,0:T(8,128)(2,1)} fusion(bf16[2,64,128,256]{3,2,1,0:T(8,128)(2,1)} %bitcast.37, s32[1024]{0:T(1024)S(1)} %pad_clamp_fusion), kind=kCustom, calls=%fused_computation | custom fusion | bytes 16777472 | tf_op jit(solution)/shard_map/jit(_take)/gather | solution.py:32
  77.8 8.8 %select_bitcast_fusion = bf16[2,64,128,256]{3,2,0,1:T(8,128)(2,1)} fusion(bf16[64,2,128,256]{3,2,1,0:T(8,128)(2,1)} %gather_fusion, pred[64]{0:T(512)(128)(4,1)S(1)} %compare_and_fusion), kind=kLoop, calls=%fused_computation.13 | loop fusion | flops 4194304 | bytes 16777280 | tf_op jit(solution)/shard_map/jit(_take)/select_n | solution.py:32
  86.6 6.0 %fusion.25 = (bf16[1,64,128,256]{3,2,0,1:T(8,128)(2,1)}, bf16[1,64,128,256]{3,2,0,1:T(8,128)(2,1)}) fusion(bf16[2,64,128,256]{3,2,0,1:T(8,128)(2,1)} %select_bitcast_fusion), kind=kLoop, calls=%fused_computation.30 | loop fusion | bytes 16777216 | tf_op jit(solution)/shard_map/slice | solution.py:34
  92.6 6.9 %reshape_squeeze.6 = bf16[4,2048,2,128]{3,2,1,0:T(2,128)(2,1)} reshape(bf16[1,64,128,256]{3,2,0,1:T(8,128)(2,1)} %get-tuple-element.5) | data formatting | bytes 8388608 | tf_op jit(solution)/shard_map/reshape;squeeze | solution.py:34
  99.5 29.1 %all-gather.5.cloned.1.call-done = bf16[4096,1024]{1,0:T(8,128)(2,1)} async-done(((bf16[1024,1024]{1,0:T(8,128)(2,1)}), bf16[4096,1024]{1,0:T(8,128)(2,1)}) %all-gather.5.cloned.1.call-update) | async-done | bytes 8388624 | tf_op jit(solution)/shard_map/all_gather | solution.py:20
  128.6 9.2 %multiply_convert_fusion = bf16[512,1024]{1,0:T(8,128)(2,1)S(1)} fusion(bf16[4096,1024]{1,0:T(8,128)(2,1)} %all-gather.5.cloned.1.call-done, bf16[512,4096]{1,0:T(8,128)(2,1)} %param.6, f32[4096]{0:T(1024)S(1)} %convert_element_type.25, f32[512]{0:T(512)S(1)} %add_rsqrt_fusion), kind=kOutput, calls=%fused_computation.22 | convolution fusion | flops 4304404480 | bytes 13649920 | tf_op jit(solution)/shard_map/dot_general | solution.py:18
  137.8 0.8 reshape.61
  138.6 6.9 %reshape_squeeze.7 = bf16[4,2048,2,128]{3,2,1,0:T(2,128)(2,1)} reshape(bf16[1,64,128,256]{3,2,0,1:T(8,128)(2,1)} %get-tuple-element.6) | data formatting | bytes 8388608 | tf_op jit(solution)/shard_map/reshape;squeeze | solution.py:35
  145.5 15.3 %bitcast_reduce_fusion = (f32[4,2,4,128]{3,2,1,0:T(4,128)S(1)}, f32[4,2,2048,128,4]{3,2,4,1,0:T(8,128)}) fusion(bf16[4,128,2,4,128]{4,3,2,1,0:T(4,128)(2,1)S(1)} %reshape.61, bf16[4,2048,2,128,1]{3,2,1,0,4:T(2,128)(2,1)} %bitcast.35), kind=kOutput, calls=%fused_computation.2 | convolution fusion | flops 2155868160 | bytes 38813696 | tf_op jit(solution)/shard_map/qrkgd,qskd->qkgrs/dot_general | solution.py:37
  160.8 13.1 %fusion.1 = f32[4,2,4,128]{3,2,1,0:T(4,128)S(1)} fusion(f32[4,2,2048,128,4]{3,2,4,1,0:T(8,128)} %get-tuple-element.8, f32[4,2,4,128]{3,2,1,0:T(4,128)S(1)} %get-tuple-element.7), kind=kLoop, calls=%fused_computation.4 | loop fusion | flops 16773120 | bytes 33587200 | tf_op jit(solution)/shard_map/reduce_sum | solution.py:42
  173.8 15.5 %fusion.16 = bf16[4,128,2,4,128]{4,1,3,2,0:T(8,128)(2,1)S(1)} fusion(bf16[4,2048,2,128,1]{3,2,1,0,4:T(2,128)(2,1)} %bitcast.36, f32[4,2,2048,128,4]{3,2,4,1,0:T(8,128)} %get-tuple-element.8, f32[4,2,4,128]{3,2,1,0:T(4,128)S(1)} %get-tuple-element.7, f32[4,128,2,4]{1,3,2,0:T(4,128)S(1)} %bitcast.38), kind=kOutput, calls=%fused_computation.21 | convolution fusion | flops 2165309440 | bytes 38830080 | tf_op jit(solution)/shard_map/qkgrs,qskd->qkgrd/dot_general | solution.py:45
  189.3 0.8 copy.18
  190.2 0.8 convert_element_type.30
  190.9 10.1 %fusion.26 = f32[512,4096]{1,0:T(8,128)} fusion(bf16[512,1024]{1,0:T(8,128)(2,1)S(1)} %convert_element_type.30, bf16[1024,4096]{1,0:T(8,128)(2,1)} %param.9), kind=kOutput, calls=%fused_computation.31 | convolution fusion | flops 4294967296 | bytes 17825792 | tf_op jit(solution)/shard_map/dot_general | solution.py:54
  201.0 0.0 reduce-scatter.2.cloned.1.call-update
  201.0 145.0 %reduce-scatter.2.cloned.1.call-done = f32[128,4096]{1,0:T(8,128)} async-done(((f32[512,4096]{1,0:T(8,128)}), f32[128,4096]{1,0:T(8,128)}) %reduce-scatter.2.cloned.1.call-update) | async-done | bytes 2097168 | tf_op jit(solution)/shard_map/reduce_scatter | solution.py:53
  346.0 2.7 convert_element_type.31
  (4 shorter events, 0.0 us)
Async XLA Ops:
  6.5 62.2 %all-gather.3.cloned.1.call-start = ((), (), s32[]{:S(2)}) async-start(), calls=%async_computation.1 | async-start | bytes 10485760 | tf_op jit(solution)/shard_map/all_gather | solution.py:30
  7.3 121.4 %all-gather.5.cloned.1.call-start = ((), (), s32[]{:S(2)}) async-start(), calls=%async_computation.2 | async-start | bytes 10485760 | tf_op jit(solution)/shard_map/all_gather | solution.py:20
  8.0 338.0 %reduce-scatter.2.cloned.1.call-start = ((), (), s32[]{:S(2)}) async-start(), calls=%async_computation.3 | async-start | bytes 10485760 | tf_op jit(solution)/shard_map/reduce_scatter | solution.py:53
Sparse Core Ops, SparseCore 0:
  8.9 59.7 all-gather.2
  70.3 58.2 all-gather.4
  201.1 144.8 reduce-scatter.1
where the time goes:
time: 357 us; the launch traced here: 355 us
  waiting for transfers between devices  231 us (65%)
  matrix products  50 us (14%)
  local copies, waits for them, and re-layouts  32.8 us (9%)
  other arithmetic  28.3 us (8%)
  between operations  13.2 us (4%)
    reduce_scatter x1, waiting for transfers between devices, per_device(): lax.psum_scatter(jnp.dot(attended, output_weight, preferred_element_type=...  145 us
    all_gather x1, waiting for transfers between devices, per_device(): whole = lax.all_gather(cache, 'corpus', axis=1, tiled=True)  55.3 us
    all_gather x1, waiting for transfers between devices, per_device(): lax.all_gather(query_weight, 'corpus', axis=0, tiled=True)  29.1 us
    dot_general x1, matrix products, per_device(): jnp.einsum('qkgrs,qskd->qkgrd', probs, values_here, preferred_element_typ...  15.5 us
    dot_general x1, matrix products, per_device(): jnp.einsum('qrkgd,qskd->qkgrs', query_tiles, keys_here, preferred_element...  15.3 us
    reduce_sum x1, other arithmetic, per_device(): totals = jnp.sum(weights, axis=-1, keepdims=True)  13.1 us
    dot_general x1, matrix products, per_device(): jnp.dot(attended, output_weight, preferred_element_type=jnp.float32)  10.1 us
    dot_general x1, matrix products, per_device(): jnp.dot(normed, lax.all_gather(query_weight, 'corpus', axis=0, tiled=True...  9.19 us
  transfers between devices with their start and end apart: 3, of which 3 were waited for; matrix products, arithmetic and copies ran while one was open for 10% of the time, Pallas kernels for 0%

commit v1 on v0

--- a/solution.py
+++ b/solution.py
@@ -1,15 +1,20 @@
+import functools
 import math
 
 import jax
 import jax.numpy as jnp
 from jax import lax
+from jax.experimental import pallas as pl
+from jax.experimental.pallas import tpu as pltpu
 from jax.sharding import PartitionSpec as P
 
 HD = 128
 BLOCK = 128
-
-
-def per_device(hidden, norm_gain, query_weight, output_weight, cache, pattern):
+PIECES = 4
+MESH = pl.DeviceIdType.MESH
+
+
+def plain_device(hidden, norm_gain, query_weight, output_weight, cache, pattern):
     widened = hidden.astype(jnp.float32)
     meansq = jnp.mean(widened * widened, axis=-1, keepdims=True)
     normed = (widened * lax.rsqrt(meansq + 1e-05) * norm_gain.astype(jnp.float32)).astype(
@@ -29,7 +34,14 @@
     slot_total = query_blocks * pattern.shape[1]
     whole = lax.all_gather(cache, "corpus", axis=1, tiled=True)
     tiles = whole.reshape(2, whole.shape[1] // BLOCK, BLOCK, kv_width)
-    picked = jnp.take(tiles, pattern.reshape(slot_total), axis=1)
+    picked = jnp.moveaxis(
+        lax.map(
+            lambda j: lax.dynamic_index_in_dim(tiles, j, axis=1, keepdims=False),
+            pattern.reshape(slot_total),
+        ),
+        0,
+        1,
+    )
     key_span = pattern.shape[1] * BLOCK
     keys_here = picked[0].reshape(query_blocks, key_span, kv_heads, HD)
     values_here = picked[1].reshape(query_blocks, key_span, kv_heads, HD)
@@ -59,7 +71,409 @@
     return summed.astype(jnp.bfloat16)
 
 
+def line_order(n):
+    table = []
+    for t in range(n):
+        ups, downs = list(range(n - 1, t, -1)), list(range(t))
+        first, second = (ups, downs) if len(ups) >= len(downs) else (downs, ups)
+        row = []
+        while first or second:
+            if first:
+                row.append(first.pop(0))
+            if second:
+                row.append(second.pop(0))
+        table.append(row + [t])
+    return table
+
+
+def layer_kernel(
+    n,
+    n_corpus,
+    hidden,
+    gain,
+    wq,
+    wo,
+    cache,
+    pattern,
+    out,
+    hid,
+    wg,
+    wov,
+    kv,
+    acc,
+    queries,
+    kbuf,
+    vbuf,
+    att,
+    part,
+    up,
+    down,
+    snd,
+    g_send,
+    g_recv,
+    l_sem,
+    r_send,
+    up_sem,
+    down_sem,
+):
+    y, c, t = lax.axis_index("dp"), lax.axis_index("corpus"), lax.axis_index("tensor")
+    x, core = c // 2, c % 2
+    c_core = x * 2 + 1 - core
+    c_x = (1 - x) * 2 + core
+    c_xc = (1 - x) * 2 + 1 - core
+    to_core, to_x, to_y = (y, c_core, t), (y, c_x, t), (1 - y, c, t)
+    to_up, to_down = (y, c, t + 1), (y, c, t - 1)
+
+    rows, kd = hid.shape[1], hid.shape[2]
+    width = wq.shape[1]
+    blk = cache.shape[1]
+
+    hid_copies = [
+        pltpu.make_async_copy(hidden.at[:, pl.ds(j * kd, kd)], hid.at[j], l_sem.at[j])
+        for j in range(n_corpus)
+    ]
+    for cp in hid_copies:
+        cp.start()
+    w_copy = pltpu.make_async_copy(wq, wg.at[c], l_sem.at[n_corpus])
+    kv_copy = pltpu.make_async_copy(cache, kv.at[:, pl.ds(c * blk, blk)], l_sem.at[n_corpus + 1])
+    ncol = wov.shape[2]
+    wo_copies = [
+        pltpu.make_async_copy(
+            wo.at[:, pl.ds(j * ncol, ncol)], wov.at[j], l_sem.at[n_corpus + 2 + j]
+        )
+        for j in range(wov.shape[0])
+    ]
+    w_copy.start()
+
+    barrier = pltpu.get_barrier_semaphore()
+    for partner in (to_core, to_x, to_y):
+        pl.semaphore_signal(barrier, inc=1, device_id=partner, device_id_type=MESH)
+
+    @pl.when(t > 0)
+    def _():
+        pl.semaphore_signal(barrier, inc=1, device_id=to_down, device_id_type=MESH)
+
+    @pl.when(t < n - 1)
+    def _():
+        pl.semaphore_signal(barrier, inc=1, device_id=to_up, device_id_type=MESH)
+
+    partners = 3 + jnp.where(t > 0, 1, 0) + jnp.where(t < n - 1, 1, 0)
+    pl.semaphore_wait(barrier, partners)
+
+    def remote(src, dst, which, kind, p, device):
+        return pltpu.make_async_remote_copy(
+            src_ref=src,
+            dst_ref=dst,
+            send_sem=g_send.at[which, kind, p],
+            recv_sem=g_recv.at[which, kind, p],
+            device_id=device,
+            device_id_type=MESH,
+        )
+
+    w_rows = kd // 2 // PIECES
+    kv_blk = blk // PIECES
+
+    def w_piece(owner, half, p):
+        return wg.at[owner, pl.ds(half * (kd // 2) + p * w_rows, w_rows)]
+
+    def kv_piece(owner, half, p):
+        first = owner * blk + half * (blk // 2) + (p % 2) * kv_blk
+        return kv.at[p // 2, pl.ds(first, kv_blk)]
+
+    def w_own(p):
+        return wq.at[pl.ds(y * (kd // 2) + p * w_rows, w_rows)]
+
+    def kv_own(p):
+        return cache.at[p // 2, pl.ds(y * (blk // 2) + (p % 2) * kv_blk, kv_blk)]
+
+    def x_send(which, p):
+        own, piece = ((w_own, w_piece), (kv_own, kv_piece))[which]
+        return remote(own(p), piece(c, y, p), which, 0, p, to_x)
+
+    def y_send(which, p):
+        piece = (w_piece, kv_piece)[which](c_x, y, p)
+        return remote(piece, piece, which, 1, p, to_y)
+
+    def cx_send(which, p):
+        piece = (w_piece, kv_piece)[which](c_x, y, p)
+        return remote(piece, piece, which, 3, p, to_core)
+
+    def cy_send(which, p):
+        piece = (w_piece, kv_piece)[which](c_x, 1 - y, p)
+        return remote(piece, piece, which, 4, p, to_core)
+
+    own_send = [
+        remote(wq, wg.at[c], 0, 2, 0, to_core),
+        remote(cache, kv.at[:, pl.ds(c * blk, blk)], 1, 2, 0, to_core),
+    ]
+
+    for p in range(PIECES):
+        x_send(0, p).start()
+    own_send[0].start()
+
+    for cp in hid_copies:
+        cp.wait()
+    tile = 32
+
+    def norm_rows(i, carry):
+        at = pl.ds(pl.multiple_of(i * tile, tile), tile)
+        total = jnp.zeros((tile, 1), jnp.float32)
+        for j in range(n_corpus):
+            wide = hid[j, at, :].astype(jnp.float32)
+            total = total + jnp.sum(wide * wide, axis=1, keepdims=True)
+        inv = lax.rsqrt(total * (1.0 / (n_corpus * kd)) + 1e-05)
+        for j in range(n_corpus):
+            wide = hid[j, at, :].astype(jnp.float32)
+            scale = gain[:, j * kd : (j + 1) * kd].astype(jnp.float32)
+            hid[j, at, :] = (wide * inv * scale).astype(jnp.bfloat16)
+        return carry
+
+    lax.fori_loop(0, rows // tile, norm_rows, 0)
+
+    n_tile = 256
+
+    def project(j, first):
+        def body(i, carry):
+            at = pl.ds(pl.multiple_of(i * n_tile, n_tile), n_tile)
+            term = jnp.dot(hid[j], wg[j, :, at], preferred_element_type=jnp.float32)
+            acc[:, at] = term if first else acc[:, at] + term
+            return carry
+
+        lax.fori_loop(0, width // n_tile, body, 0)
+
+    w_copy.wait()
+    project(c, True)
+    kv_copy.start()
+    own_send[1].start()
+    for cp in wo_copies:
+        cp.start()
+
+    for p in range(PIECES):
+        x_send(0, p).wait_recv()
+        y_send(0, p).start()
+        cx_send(0, p).start()
+        x_send(1, p).start()
+    own_send[0].wait_recv()
+    project(c_core, False)
+    for p in range(PIECES):
+        y_send(0, p).wait_recv()
+        cy_send(0, p).start()
+    project(c_x, False)
+    for p in range(PIECES):
+        cx_send(0, p).wait_recv()
+        cy_send(0, p).wait_recv()
+    project(c_xc, False)
+    heads = width // HD
+    kv_heads = kv.shape[3] // HD
+    group = heads // kv_heads
+    blocks = rows // BLOCK
+    for b in range(blocks):
+        for h in range(heads):
+            term = acc[b * BLOCK : (b + 1) * BLOCK, h * HD : (h + 1) * HD]
+            queries[b, h] = (term * (1.0 / math.sqrt(HD))).astype(jnp.bfloat16)
+
+    for p in range(PIECES):
+        x_send(1, p).wait_recv()
+        y_send(1, p).start()
+        cx_send(1, p).start()
+    for p in range(PIECES):
+        y_send(1, p).wait_recv()
+        cy_send(1, p).start()
+    kv_copy.wait()
+    own_send[1].wait_recv()
+    for p in range(PIECES):
+        cx_send(1, p).wait_recv()
+        cy_send(1, p).wait_recv()
+    for cp in wo_copies:
+        cp.wait()
+
+    slots = pattern.shape[1]
+    together = 2
+    table = line_order(n)
+    n_parts = wov.shape[0]
+
+    def passes(b, j):
+        return pltpu.make_async_remote_copy(
+            src_ref=snd.at[b, j],
+            dst_ref=up.at[b, j],
+            send_sem=r_send.at[b, j],
+            recv_sem=up_sem.at[b, j],
+            device_id=to_up,
+            device_id_type=MESH,
+        )
+
+    def passes_down(b, j):
+        return pltpu.make_async_remote_copy(
+            src_ref=snd.at[b, j],
+            dst_ref=down.at[b, j],
+            send_sem=r_send.at[b, j],
+            recv_sem=down_sem.at[b, j],
+            device_id=to_down,
+            device_id_type=MESH,
+        )
+
+    def one_block(step, carry):
+        b = 0
+        for i in range(n):
+            for s in range(n):
+                b = jnp.where((t == i) & (step == s), table[i][s], b)
+
+        def pick(s, carry):
+            block = pattern[b, s]
+            at = pl.ds(pl.multiple_of(s * BLOCK, BLOCK), BLOCK)
+            for h in range(kv_heads):
+                kbuf[h, at, :] = kv[0, block, :, h * HD : (h + 1) * HD]
+                vbuf[h, at, :] = kv[1, block, :, h * HD : (h + 1) * HD]
+            return carry
+
+        lax.fori_loop(0, slots, pick, 0)
+
+        def attend(i, carry):
+            h = i * together // group
+            q = queries[b, pl.ds(i * together, together)].reshape(together * BLOCK, HD)
+            scores = lax.dot_general(
+                q, kbuf[h], (((1,), (1,)), ((), ())), preferred_element_type=jnp.float32
+            )
+            weights = jnp.exp(scores - jnp.max(scores, axis=1, keepdims=True))
+            totals = jnp.sum(weights, axis=1, keepdims=True)
+            mixed = jnp.dot(
+                weights.astype(jnp.bfloat16), vbuf[h], preferred_element_type=jnp.float32
+            )
+            mixed = (mixed / totals).astype(jnp.bfloat16)
+            att[pl.ds(i * together, together)] = mixed.reshape(together, BLOCK, HD)
+            return carry
+
+        lax.fori_loop(0, heads // together, attend, 0)
+
+        def send_part(j, carry):
+            left = jnp.concatenate([att[h] for h in range(heads)], axis=1)
+            part[...] = jnp.dot(left, wov[j], preferred_element_type=jnp.float32)
+
+            @pl.when((t > 0) & (b >= t))
+            def _():
+                passes(b, j).wait_recv()
+                part[...] += up[b, j].astype(jnp.float32)
+
+            @pl.when((t < n - 1) & (b <= t))
+            def _():
+                passes_down(b, j).wait_recv()
+                part[...] += down[b, j].astype(jnp.float32)
+
+            @pl.when(b > t)
+            def _():
+                snd[b, j] = part[...].astype(jnp.bfloat16)
+                passes(b, j).start()
+
+            @pl.when(b < t)
+            def _():
+                snd[b, j] = part[...].astype(jnp.bfloat16)
+                passes_down(b, j).start()
+
+            @pl.when(b == t)
+            def _():
+                out[:, pl.ds(pl.multiple_of(j * ncol, ncol), ncol)] = part[...].astype(
+                    jnp.bfloat16
+                )
+
+            return carry
+
+        lax.fori_loop(0, n_parts, send_part, 0)
+        return carry
+
+    lax.fori_loop(0, blocks, one_block, 0)
+
+    for which in range(2):
+        own_send[which].wait_send()
+        for p in range(PIECES):
+            for send in (x_send, y_send, cx_send, cy_send):
+                send(which, p).wait_send()
+
+    def finish(i, carry):
+        b, j = i // n_parts, i % n_parts
+
+        @pl.when(b > t)
+        def _():
+            passes(b, j).wait_send()
+
+        @pl.when(b < t)
+        def _():
+            passes_down(b, j).wait_send()
+
+        return carry
+
+    lax.fori_loop(0, blocks * n_parts, finish, 0)
+
+
+def fused_device(n, n_corpus, hidden, norm_gain, query_weight, output_weight, cache, pattern):
+    rows, features = hidden.shape
+    kd, width = query_weight.shape
+    columns = output_weight.shape[1]
+    kv_width = cache.shape[2]
+    blk = cache.shape[1] // BLOCK
+    heads = width // HD
+    kv_heads = kv_width // HD
+    blocks = rows // BLOCK
+    span = pattern.shape[1] * BLOCK
+    n_parts = 4
+    ncol = columns // n_parts
+    bf16, f32 = jnp.bfloat16, jnp.float32
+    anywhere = pl.BlockSpec(memory_space=pl.ANY)
+    vmem = pl.BlockSpec(memory_space=pltpu.VMEM)
+    return pl.pallas_call(
+        functools.partial(layer_kernel, n, n_corpus),
+        out_shape=jax.ShapeDtypeStruct((rows // n, columns), bf16),
+        in_specs=[
+            anywhere,
+            vmem,
+            anywhere,
+            anywhere,
+            anywhere,
+            pl.BlockSpec(memory_space=pltpu.SMEM),
+        ],
+        out_specs=vmem,
+        scratch_shapes=[
+            pltpu.VMEM((n_corpus, rows, kd), bf16),
+            pltpu.VMEM((n_corpus, kd, width), bf16),
+            pltpu.VMEM((n_parts, width, ncol), bf16),
+            pltpu.VMEM((2, n_corpus * blk, BLOCK, kv_width), bf16),
+            pltpu.VMEM((rows, width), f32),
+            pltpu.VMEM((blocks, heads, BLOCK, HD), bf16),
+            pltpu.VMEM((kv_heads, span, HD), bf16),
+            pltpu.VMEM((kv_heads, span, HD), bf16),
+            pltpu.VMEM((heads, BLOCK, HD), bf16),
+            pltpu.VMEM((BLOCK, ncol), f32),
+            pltpu.VMEM((n, n_parts, BLOCK, ncol), bf16),
+            pltpu.VMEM((n, n_parts, BLOCK, ncol), bf16),
+            pltpu.VMEM((n, n_parts, BLOCK, ncol), bf16),
+            pltpu.SemaphoreType.DMA((2, 5, PIECES)),
+            pltpu.SemaphoreType.DMA((2, 5, PIECES)),
+            pltpu.SemaphoreType.DMA((n_corpus + 2 + n_parts,)),
+            pltpu.SemaphoreType.DMA((n, n_parts)),
+            pltpu.SemaphoreType.DMA((n, n_parts)),
+            pltpu.SemaphoreType.DMA((n, n_parts)),
+        ],
+        compiler_params=pltpu.CompilerParams(
+            collective_id=0, has_side_effects=True, vmem_limit_bytes=60 * 1024 * 1024
+        ),
+    )(
+        hidden,
+        norm_gain.reshape(1, features),
+        query_weight,
+        output_weight,
+        cache.reshape(2, blk, BLOCK, kv_width),
+        pattern,
+    )
+
+
 def solution(mesh):
+    n_dp, n_corpus, n = mesh.shape["dp"], mesh.shape["corpus"], mesh.shape["tensor"]
+
+    def per_device(hidden, norm_gain, query_weight, output_weight, cache, pattern):
+        args = (hidden, norm_gain, query_weight, output_weight, cache, pattern)
+        if n_dp == 2 and n_corpus == 4 and hidden.shape[0] == n * BLOCK:
+            return fused_device(n, n_corpus, *args)
+        return plain_device(*args)
+
     in_specs = (
         P(("dp", "corpus"), None),
         P(),

time: 357 us -> 144 us (0.40)
  waiting for transfers between devices: 231 us -> 0 us
  Pallas kernels: 0 us -> 140 us
  matrix products: 50 us -> 0 us
  local copies, waits for them, and re-layouts: 32.8 us -> 3.6 us
  other arithmetic: 28.3 us -> 0 us
  between operations: 13.2 us -> 0.01 us
    reduce_scatter x1 -> x0, waiting for transfers between devices: 145 us -> none  [per_device(): lax.psum_scatter(jnp.dot(attended, output_weight, preferred_element_type=...]
    pallas_call x0 -> x1, Pallas kernels: none -> 140 us  [fused_device(): pl.pallas_call(functools.partial(layer_kernel, n, n_corpus), out_shape=ja...]
    all_gather x2 -> x0, waiting for transfers between devices: 84.4 us -> none  [the longest x1 55.3 us: per_device(): whole = lax.all_gather(cache, 'corpus', axis=1, tiled=True)]
    dot_general x4 -> x0, matrix products: 50 us -> none  [the longest x1 15.5 us: per_device(): jnp.einsum('qkgrs,qskd->qkgrd', probs, values_here, preferred_element_typ...]
    reduce_sum x2 -> x0, other arithmetic: 16.1 us -> none  [the longest x1 13.1 us: per_device(): totals = jnp.sum(weights, axis=-1, keepdims=True)]
    another operation x2 -> x0, local copies, waits for them, and re-layouts: 13.9 us -> none  [the longest x1 6.93 us: per_device(): values_here = picked[1].reshape(query_blocks, key_span, kv_heads, HD)]
    gather x1 -> x0, local copies, waits for them, and re-layouts: 9.07 us -> none  [per_device(): picked = jnp.take(tiles, pattern.reshape(slot_total), axis=1)]
    select_n x2 -> x0, other arithmetic: 8.77 us -> none  [per_device(): picked = jnp.take(tiles, pattern.reshape(slot_total), axis=1)]
  transfers between devices with their start and end apart: 3 -> 0, of which waited for: 3 -> 0; matrix products, arithmetic and copies ran while one was open for 10% -> 0% of each run, Pallas kernels for 0% -> 0%
where the time goes in v1:
time: 144 us; the launch traced here: 143 us
  Pallas kernels  140 us (97%)
  local copies, waits for them, and re-layouts  3.6 us (2%)
    pallas_call x1, Pallas kernels, fused_device(): pl.pallas_call(functools.partial(layer_kernel, n, n_corpus), out_shape=ja...  140 us

profile of v1, /device:TPU:17, one launch (start us, length us, event | category | flops | bytes accessed | tf_op | source)
XLA Modules:
  0.0 143.4 jit_solution(7781425580699021539)
XLA Ops:
  0.0 1.3 reshape.6.gain
  1.3 139.8 %shard_map.64 = bf16[128,4096]{1,0:T(8,128)(2,1)} custom-call(bf16[512,4096]{1,0:T(8,128)(2,1)} %hidden.1, bf16[1,4096]{1,0:T(2,128)(2,1)} %reshape.6.gain, bf16[1024,1024]{1,0:T(8,128)(2,1)} %wq.1, bf16[1024,4096]{1,0:T(8,128)(2,1)} %wo.1, bf16[2,16,128,256]{3,2,1,0:T(8,128)(2,1)} %bitcast.1, s32[4,16]{1,0:T(4,128)} %pattern.1), custom_call_target="tpu_custom_call" | custom-call | tf_op jit(solution)/shard_map/pallas_call | solution.py:422
  141.1 2.3 %copy.8 = bf16[128,4096]{1,0:T(8,128)(2,1)} copy(bf16[128,4096]{1,0:T(8,128)(2,1)} %shard_map.64) | data formatting | bytes 2097152

commit v2 on v1

--- a/solution.py
+++ b/solution.py
@@ -10,7 +10,7 @@
 
 HD = 128
 BLOCK = 128
-PIECES = 4
+PIECES = 8
 MESH = pl.DeviceIdType.MESH
 
 
@@ -177,14 +177,15 @@
         return wg.at[owner, pl.ds(half * (kd // 2) + p * w_rows, w_rows)]
 
     def kv_piece(owner, half, p):
-        first = owner * blk + half * (blk // 2) + (p % 2) * kv_blk
-        return kv.at[p // 2, pl.ds(first, kv_blk)]
+        first = owner * blk + half * (blk // 2) + (p % (PIECES // 2)) * kv_blk
+        return kv.at[p // (PIECES // 2), pl.ds(first, kv_blk)]
 
     def w_own(p):
         return wq.at[pl.ds(y * (kd // 2) + p * w_rows, w_rows)]
 
     def kv_own(p):
-        return cache.at[p // 2, pl.ds(y * (blk // 2) + (p % 2) * kv_blk, kv_blk)]
+        half = PIECES // 2
+        return cache.at[p // half, pl.ds(y * (blk // 2) + (p % half) * kv_blk, kv_blk)]
 
     def x_send(which, p):
         own, piece = ((w_own, w_piece), (kv_own, kv_piece))[which]
@@ -414,7 +415,7 @@
     kv_heads = kv_width // HD
     blocks = rows // BLOCK
     span = pattern.shape[1] * BLOCK
-    n_parts = 4
+    n_parts = 8
     ncol = columns // n_parts
     bf16, f32 = jnp.bfloat16, jnp.float32
     anywhere = pl.BlockSpec(memory_space=pl.ANY)

time: 144 us -> 143 us (level)
  no operation moved by 1% of the time
where the time goes in v2:
time: 143 us
  Pallas kernels  139 us (97%)
  local copies, waits for them, and re-layouts  3.6 us (3%)
    pallas_call x1, Pallas kernels, fused_device(): pl.pallas_call(functools.partial(layer_kernel, n, n_corpus), out_shape=ja...  139 us

profile of v2, /device:TPU:17, one launch (start us, length us, event | category | flops | bytes accessed | tf_op | source)
XLA Modules:
  0.0 143.0 jit_solution(3067928611922369690)
XLA Ops:
  0.0 1.3 reshape.6.gain
  1.3 139.4 %shard_map.64 = bf16[128,4096]{1,0:T(8,128)(2,1)} custom-call(bf16[512,4096]{1,0:T(8,128)(2,1)} %hidden.1, bf16[1,4096]{1,0:T(2,128)(2,1)} %reshape.6.gain, bf16[1024,1024]{1,0:T(8,128)(2,1)} %wq.1, bf16[1024,4096]{1,0:T(8,128)(2,1)} %wo.1, bf16[2,16,128,256]{3,2,1,0:T(8,128)(2,1)} %bitcast.1, s32[4,16]{1,0:T(4,128)} %pattern.1), custom_call_target="tpu_custom_call" | custom-call | tf_op jit(solution)/shard_map/pallas_call | solution.py:423
  140.7 2.3 %copy.8 = bf16[128,4096]{1,0:T(8,128)(2,1)} copy(bf16[128,4096]{1,0:T(8,128)(2,1)} %shard_map.64) | data formatting | bytes 2097152
